TPU v7x, 32 devices: a whole 2x2x4 slice. The times are simulated.
32 devices in a mesh: groups: 2 (over x), ptcl: 8 (over z, y), vol: 2 (over core).
Axes of the slice: x: 2, y: 2, z: 4, core: 2. Of those that a mesh axis runs over, the one named last changes fastest.
Arguments:
- reference_slabs: bfloat16 [8, 180, 5760], P('groups', 'vol'), parts along dimension 0, may hold values from -0.03125 to 0.03125
- slice_table: bfloat16 [128, 180], replicated, may hold values from -4 to 4
- images: bfloat16 [1536, 5760], P(('groups', 'ptcl'), 'vol'), parts along dimension 0, may hold values from -16 to 16
- offsets: float32 [1536, 16], P(('groups', 'ptcl')), parts along dimension 0, may hold values from -8 to 250
- orient_lists: int32 [1536, 16], P(('groups', 'ptcl')), parts along dimension 0, may hold values from 0 to 511
- counts: int32 [1536], P(('groups', 'ptcl')), parts along dimension 0, may hold values from 1 to 16, 6528 in all
Outputs:
- new_ref: bfloat16 [8, 180, 5760], P('groups', None, 'vol'), parts along dimension 0
- log_norm: float32 [1536], P(('groups', 'ptcl')), parts along dimension 0
There are 2 independent parts, one for each index of `groups`. A program takes and returns all parts, laid end to end along the dimension named above; an argument that names none is the same for every part. Nothing has to cross between parts.
All inputs are finite; a program needn't handle non-finite values. No bound on the sum of `counts` on one device may be relied on, other than what follows from the above.
Results may differ from a plain program's by a relative error of at most 0.0079.
Values may be sent and summed in bfloat16 or wider, within the bound.
A program may use at most 128 MiB of HBM per device.

v0:
```python
import math

import jax
import jax.numpy as jnp
from jax import lax
from jax.sharding import PartitionSpec as P


def posterior(sel_cross, sel_power, offsets, counts, score_scale):
    scores = score_scale * (sel_cross - 0.5 * sel_power) + offsets
    slot_ids = jnp.arange(scores.shape[1], dtype=jnp.int32)
    live_slots = slot_ids[None, :] < counts[:, None]
    masked = jnp.where(live_slots, scores, jnp.float32(-1e30))
    row_top = jnp.max(masked, axis=1, keepdims=True)
    expon = jnp.where(live_slots, jnp.exp(masked - row_top), jnp.float32(0.0))
    row_total = jnp.sum(expon, axis=1, keepdims=True)
    weights = expon / row_total
    log_norm = (row_top + jnp.log(row_total))[:, 0]
    return (weights, log_norm)


def spread_weights(weights, orient_lists, columns):
    targets = jnp.arange(columns, dtype=jnp.int32)
    spread_sum = jnp.zeros((weights.shape[0], columns), jnp.float32)
    for slot in range(weights.shape[1]):
        hits = (orient_lists[:, slot : slot + 1] == targets[None, :]).astype(jnp.float32)
        spread_sum = spread_sum + weights[:, slot : slot + 1] * hits
    return spread_sum.astype(jnp.bfloat16)


def back_project(sum_rows, totals, slice_table, classes):
    orients = slice_table.shape[0]
    stacked = sum_rows.reshape(classes, orients, sum_rows.shape[1])
    numerator = jnp.einsum("ok,cop->ckp", slice_table, stacked, preferred_element_type=jnp.float32)
    kernel = slice_table.astype(jnp.float32)
    denominator = 1.0 + jnp.einsum(
        "ok,co->ck",
        kernel * kernel,
        totals.reshape(classes, orients),
        precision=lax.Precision.HIGHEST,
    )
    return (numerator / denominator[:, :, None]).astype(jnp.bfloat16)


def on_device(reference_slabs, slice_table, images, offsets, orient_lists, counts):
    classes = reference_slabs.shape[0]
    kz_dev = reference_slabs.shape[1]
    orients = slice_table.shape[0]
    half_pixels = images.shape[1]
    columns = classes * orients
    table_local = lax.dynamic_slice_in_dim(slice_table, lax.axis_index("vol") * kz_dev, kz_dev, 1)
    partial_value = jnp.einsum(
        "ckp,ok->pco", reference_slabs, table_local, preferred_element_type=jnp.float32
    )
    projection = lax.psum_scatter(
        partial_value.reshape(lax.axis_size("vol") * half_pixels, columns),
        "vol",
        scatter_dimension=0,
        tiled=True,
    ).astype(jnp.bfloat16)
    proj_wide = projection.astype(jnp.float32)
    power_part = jnp.sum(proj_wide * proj_wide, axis=0)
    cross_part = jnp.dot(images, projection, preferred_element_type=jnp.float32)
    crossed, powers = lax.psum((cross_part, power_part), "vol")
    sel_cross = jnp.take_along_axis(crossed, orient_lists, axis=1)
    sel_power = powers[orient_lists]
    score_scale = 4.0 / math.sqrt(half_pixels * lax.axis_size("vol"))
    weights, log_norm = posterior(sel_cross, sel_power, offsets, counts, score_scale)
    spread = spread_weights(weights, orient_lists, columns)
    row_part = lax.dot_general(
        spread, images, (((0,), (0,)), ((), ())), preferred_element_type=jnp.float32
    )
    total_part = jnp.sum(spread.astype(jnp.float32), axis=0)
    sum_rows, totals = lax.psum((row_part, total_part), "ptcl")
    new_ref = back_project(sum_rows.astype(jnp.bfloat16), totals, slice_table, classes)
    return (new_ref, log_norm)


def solution(mesh):
    placed = (
        P("groups", "vol", None),
        P(),
        P(("groups", "ptcl"), "vol"),
        P(("groups", "ptcl"), None),
        P(("groups", "ptcl"), None),
        P(("groups", "ptcl")),
    )
    return jax.shard_map(
        on_device,
        mesh=mesh,
        in_specs=placed,
        out_specs=(P("groups", None, "vol"), P(("groups", "ptcl"))),
        check_vma=False,
    )
```

profile of v0, /device:TPU:0, one launch (start us, length us, event | category | flops | bytes accessed | tf_op | source)
XLA Modules:
  0.0 348.7 jit_solution(11395343727582568166)
XLA Ops:
  7.2 0.0 copy-start
  7.2 0.0 reduce-scatter.4.cloned.1.call-start
  7.2 8.2 %fusion = f32[128,4,5760]{2,0,1:T(8,128)} fusion(bf16[4,90,5760]{2,0,1:T(4,128)(2,1)} %param.6, bf16[128,180]{0,1:T(8,128)(2,1)} %param.7, s32[]{:T(128)S(6)} %select_n.20), kind=kOutput, calls=%fused_computation.4 | convolution fusion | flops 530841600 | bytes 15968260 | tf_op jit(solution)/shard_map/ckp,ok->pco/dot_general | solution.py:52
  15.5 12.3 %copy.54 = f32[5760,512]{1,0:T(8,128)} copy(f32[5760,512]{0,1:T(8,128)} %bitcast.96) | data formatting | bytes 23592960
  27.8 0.0 copy-start.1
  27.8 0.0 reduce-scatter.4.cloned.1.call-update
  27.8 0.0 all-reduce.4.cloned.1.call-start
  27.9 0.6 copy-done.1
  28.5 0.1 copy.48
  28.6 0.1 reshape.42
  28.7 0.1 copy.50
  28.8 0.1 reshape.36
  28.9 22.3 %reduce-scatter.4.cloned.1.call-done = f32[2880,512]{1,0:T(8,128)} async-done(((f32[5760,512]{1,0:T(8,128)}), f32[2880,512]{1,0:T(8,128)}) %reduce-scatter.4.cloned.1.call-update) | async-done | bytes 5898256
  51.1 5.2 %copy.55 = bf16[2880,512]{0,1:T(8,128)(2,1)} copy(f32[2880,512]{1,0:T(8,128)} %reduce-scatter.4.cloned.1.call-done) | data formatting | bytes 8847360
  56.4 2.5 multiply_reduce_fusion
  58.9 0.0 copy-done
  58.9 3.6 %fusion.7 = f32[96,512]{1,0:T(8,128)} fusion(bf16[96,2880]{1,0:T(8,128)(2,1)S(1)} %copy-done, bf16[2880,512]{0,1:T(8,128)(2,1)} %copy.55), kind=kOutput, calls=%fused_computation.12 | convolution fusion | flops 283115520 | bytes 3698688 | tf_op jit(solution)/shard_map/dot_general | solution.py:63
  62.5 0.0 all-reduce.4.cloned.1.call-update
  62.5 2.5 psum.29
  65.0 9.5 %gather_fusion = f32[1536]{0:T(1024)S(1)} fusion(f32[512]{0:T(512)S(1)} %psum.29, s32[2048]{0:T(1024)S(1)} %pad_clamp_fusion), kind=kCustom, calls=%fused_computation | custom fusion | bytes 18432 | tf_op jit(solution)/shard_map/gather | solution.py:66
  74.5 0.1 reshape.51
  74.5 0.1 copy.51
  74.6 0.0 copy-start.3
  74.6 0.0 copy-start.4
  74.6 7.4 %all-reduce.4.cloned.1.call-done = f32[96,512]{1,0:T(8,128)} async-done(((f32[96,512]{1,0:T(8,128)}), f32[96,512]{1,0:T(8,128)}) %all-reduce.4.cloned.1.call-update) | async-done | bytes 196624 | tf_op jit(solution)/shard_map/psum | solution.py:64
  82.0 11.5 %gather_fusion.1 = f32[1536]{0:T(1024)S(1)} fusion(f32[96,512]{1,0:T(8,128)} %all-reduce.4.cloned.1.call-done, s32[1536]{0:T(1024)S(1)} %reshape.42), kind=kCustom, calls=%fused_computation.1 | custom fusion | bytes 24576 | tf_op jit(solution)/shard_map/jit(take_along_axis)/gather | solution.py:65
  93.5 0.1 reshape.45
  93.6 0.1 copy.49
  93.7 0.0 copy-done.3
  93.7 0.0 copy-done.4
  93.8 4.1 %fusion.18 = f32[512,2880]{0,1:T(8,128)} fusion(bf16[96,2880]{1,0:T(8,128)(2,1)S(1)} %copy-done, f32[96]{0:T(128)S(1)} %get-tuple-element.35, s32[96]{0:T(128)S(1)} %get-tuple-element.32, f32[96]{0:T(128)S(1)} %get-tuple-element.36, s32[96]{0:T(128)S(1)} %get-tuple-element.33, f32[96]{0:T(128)S(1)} %get-tuple-element.37, s32[96]{0:T(128)S(1)} %get-tuple-element.31, ...), kind=kOutput, calls=%fused_computation.80 | convolution fusion | flops 285474816 | bytes 6463488 | tf_op jit(solution)/shard_map/dot_general | solution.py:70
  97.9 0.0 copy-start.2
  97.9 0.6 convert_reduce_fusion
  98.4 0.5 log_add_fusion
  99.0 235.2 %all-reduce.5 = (f32[4,128]{1,0:T(4,128)S(1)}, bf16[512,2880]{0,1:T(8,128)(2,1)}) all-reduce(f32[4,128]{1,0:T(4,128)S(1)} %bitcast.97, f32[512,2880]{0,1:T(8,128)} %fusion.18), channel_id=1, replica_groups=mesh['groups'=2,'ptcl'=8,'vol'=2] {'ptcl'}, use_global_device_ids=true, to_apply=%region_8.9 | all-reduce | flops 1475072 | bytes 8851456 | tf_op jit(solution)/shard_map/psum | solution.py:74
  334.1 0.0 copy-done.2
  334.1 0.2 convolution_add_fusion
  334.4 3.8 %fusion.2 = bf16[4,180,2880]{2,1,0:T(8,128)(2,1)S(1)} fusion(f32[4,180]{1,0:T(4,128)S(1)} %convolution_add_fusion, bf16[128,180]{0,1:T(8,128)(2,1)S(1)} %copy-done.2, bf16[512,2880]{0,1:T(8,128)(2,1)} %get-tuple-element.15), kind=kOutput, calls=%fused_computation.6 | convolution fusion | flops 534988800 | bytes 7145280 | tf_op jit(solution)/shard_map/ok,cop->ckp/dot_general | solution.py:34
  338.2 3.7 %copy.53 = bf16[4,180,2880]{2,0,1:T(4,128)(2,1)} copy(bf16[4,180,2880]{2,1,0:T(8,128)(2,1)S(1)} %fusion.2) | data formatting | bytes 8294400
  (9 shorter events, 0.1 us)
Async XLA Ops:
  7.2 51.7 %copy-start = (bf16[96,2880]{1,0:T(8,128)(2,1)S(1)}, bf16[96,2880]{1,0:T(8,128)(2,1)}, u32[]{:S(2)}) copy-start(bf16[96,2880]{1,0:T(8,128)(2,1)} %param.8) | copy-start | bytes 1658884
  7.2 44.0 %reduce-scatter.4.cloned.1.call-start = ((), (), s32[]{:S(2)}) async-start(), calls=%async_computation.2 | async-start | bytes 17694720
  27.8 0.7 copy-start.1
  27.8 54.2 %all-reduce.4.cloned.1.call-start = ((), (), s32[]{:S(2)}) async-start(), calls=%async_computation.1 | async-start | bytes 393216 | tf_op jit(solution)/shard_map/psum | solution.py:64
  74.6 19.1 %copy-start.3 = (f32[96,16]{0,1:T(8,128)S(1)}, f32[96,16]{0,1:T(8,128)}, u32[]{:S(2)}) copy-start(f32[96,16]{0,1:T(8,128)} %param.9) | copy-start | bytes 18436
  74.6 19.1 %copy-start.4 = (s32[96]{0:T(128)S(1)}, s32[96]{0:T(128)}, u32[]{:S(2)}) copy-start(s32[96]{0:T(128)} %param.11) | copy-start | bytes 1156
  97.9 236.3 %copy-start.2 = (bf16[128,180]{0,1:T(8,128)(2,1)S(1)}, bf16[128,180]{0,1:T(8,128)(2,1)}, u32[]{:S(2)}) copy-start(bf16[128,180]{0,1:T(8,128)(2,1)} %param.7) | copy-start | bytes 138244
Sparse Core Ops, SparseCore 0:
  27.9 23.1 reduce-scatter.3
  62.6 19.3 all-reduce.3
where the time goes:
time: 349 us
  blocking collectives  238 us (68%)
  local copies, waits for them, and re-layouts  43.5 us (12%)
  waiting for transfers between devices  29.7 us (9%)
  matrix products  19.9 us (6%)
  between operations  14.2 us (4%)
  other arithmetic  3.72 us (1%)
    psum x1, blocking collectives, on_device(): sum_rows, totals = lax.psum((row_part, total_part), 'ptcl')  235 us
    unnamed x3, waiting for transfers between devices  22.3 us
    unnamed x13, local copies, waits for them, and re-layouts  21.8 us
    gather x5, local copies, waits for them, and re-layouts, on_device(): sel_cross = jnp.take_along_axis(crossed, orient_lists, axis=1)  11.8 us
    gather x1, local copies, waits for them, and re-layouts, on_device(): sel_power = powers[orient_lists]  9.47 us
    dot_general x1, matrix products, on_device(): jnp.einsum('ckp,ok->pco', reference_slabs, table_local, preferred_element...  8.25 us
    psum x1, waiting for transfers between devices, on_device(): crossed, powers = lax.psum((cross_part, power_part), 'vol')  7.38 us
  transfers between devices with their start and end apart: 2, of which 2 were waited for; matrix products, arithmetic and copies ran while one was open for 3% of the time, Pallas kernels for 0%

commit v1 on v0

--- a/solution.py
+++ b/solution.py
@@ -6,8 +6,8 @@
 from jax.sharding import PartitionSpec as P
 
 
-def posterior(sel_cross, sel_power, offsets, counts, score_scale):
-    scores = score_scale * (sel_cross - 0.5 * sel_power) + offsets
+def posterior(half_scores, offsets, counts, score_scale):
+    scores = score_scale * half_scores + offsets
     slot_ids = jnp.arange(scores.shape[1], dtype=jnp.int32)
     live_slots = slot_ids[None, :] < counts[:, None]
     masked = jnp.where(live_slots, scores, jnp.float32(-1e30))
@@ -43,35 +43,38 @@
 
 
 def on_device(reference_slabs, slice_table, images, offsets, orient_lists, counts):
-    classes = reference_slabs.shape[0]
-    kz_dev = reference_slabs.shape[1]
+    classes, kz_dev, pixels = reference_slabs.shape
     orients = slice_table.shape[0]
     half_pixels = images.shape[1]
     columns = classes * orients
-    table_local = lax.dynamic_slice_in_dim(slice_table, lax.axis_index("vol") * kz_dev, kz_dev, 1)
-    partial_value = jnp.einsum(
-        "ckp,ok->pco", reference_slabs, table_local, preferred_element_type=jnp.float32
+    halves = lax.axis_size("vol")
+    vol = lax.axis_index("vol")
+    all_images = lax.all_gather(images, "ptcl", axis=0, tiled=True)
+    low, high = reference_slabs[:, :, :half_pixels], reference_slabs[:, :, half_pixels:]
+    first = vol == 0
+    mine = jnp.where(first, low, high)
+    other = lax.ppermute(jnp.where(first, high, low), "vol", [(0, 1), (1, 0)])
+    table_mine = jnp.where(first, slice_table[:, :kz_dev], slice_table[:, kz_dev:])
+    table_other = jnp.where(first, slice_table[:, kz_dev:], slice_table[:, :kz_dev])
+    projection = (
+        jnp.einsum("ok,ckp->cop", table_mine, mine, preferred_element_type=jnp.float32)
+        + jnp.einsum("ok,ckp->cop", table_other, other, preferred_element_type=jnp.float32)
+    ).astype(jnp.bfloat16).reshape(columns, half_pixels)
+    proj_wide = projection.astype(jnp.float32)
+    power_part = jnp.sum(proj_wide * proj_wide, axis=1)
+    cross_part = lax.dot_general(images, projection, (((1,), (1,)), ((), ())), preferred_element_type=jnp.float32)
+    joint = cross_part - 0.5 * power_part[None, :]
+    targets = jnp.arange(columns, dtype=jnp.int32)
+    sel = jnp.sum(jnp.where(orient_lists[:, :, None] == targets[None, None, :], joint[:, None, :], 0.0), axis=2)
+    sel = lax.psum(sel, "vol")
+    score_scale = 4.0 / math.sqrt(half_pixels * halves)
+    weights, log_norm = posterior(sel, offsets, counts, score_scale)
+    spread = spread_weights(weights, orient_lists, columns)
+    all_spread = lax.all_gather(spread, "ptcl", axis=0, tiled=True)
+    sum_rows = lax.dot_general(
+        all_spread, all_images, (((0,), (0,)), ((), ())), preferred_element_type=jnp.float32
     )
-    projection = lax.psum_scatter(
-        partial_value.reshape(lax.axis_size("vol") * half_pixels, columns),
-        "vol",
-        scatter_dimension=0,
-        tiled=True,
-    ).astype(jnp.bfloat16)
-    proj_wide = projection.astype(jnp.float32)
-    power_part = jnp.sum(proj_wide * proj_wide, axis=0)
-    cross_part = jnp.dot(images, projection, preferred_element_type=jnp.float32)
-    crossed, powers = lax.psum((cross_part, power_part), "vol")
-    sel_cross = jnp.take_along_axis(crossed, orient_lists, axis=1)
-    sel_power = powers[orient_lists]
-    score_scale = 4.0 / math.sqrt(half_pixels * lax.axis_size("vol"))
-    weights, log_norm = posterior(sel_cross, sel_power, offsets, counts, score_scale)
-    spread = spread_weights(weights, orient_lists, columns)
-    row_part = lax.dot_general(
-        spread, images, (((0,), (0,)), ((), ())), preferred_element_type=jnp.float32
-    )
-    total_part = jnp.sum(spread.astype(jnp.float32), axis=0)
-    sum_rows, totals = lax.psum((row_part, total_part), "ptcl")
+    totals = jnp.sum(all_spread.astype(jnp.float32), axis=0)
     new_ref = back_project(sum_rows.astype(jnp.bfloat16), totals, slice_table, classes)
     return (new_ref, log_norm)
 

time: 349 us -> 116 us (0.33)
  blocking collectives: 238 us -> 40.1 us
  local copies, waits for them, and re-layouts: 43.5 us -> 7.81 us
  matrix products: 19.9 us -> 14.7 us
  other arithmetic: 3.72 us -> 7.68 us
    psum x2 -> x1, blocking collectives: 238 us -> 3.72 us  [on_device(): sel = lax.psum(sel, 'vol')]
    all_gather x0 -> x1, blocking collectives: none -> 36.3 us  [on_device(): all_spread = lax.all_gather(spread, 'ptcl', axis=0, tiled=True)]
    all_gather x0 -> x1, waiting for transfers between devices: none -> 27.7 us  [on_device(): all_images = lax.all_gather(images, 'ptcl', axis=0, tiled=True)]
    unnamed x3 -> x1, waiting for transfers between devices: 22.3 us -> 0.68 us
    gather x6 -> x0, local copies, waits for them, and re-layouts: 21.3 us -> none  [the longest x5 11.8 us: on_device(): sel_cross = jnp.take_along_axis(crossed, orient_lists, axis=1)]
    unnamed x13 -> x11, local copies, waits for them, and re-layouts: 21.8 us -> 3.86 us
    psum x1 -> x0, waiting for transfers between devices: 7.38 us -> none  [on_device(): crossed, powers = lax.psum((cross_part, power_part), 'vol')]
    select_n x1, other arithmetic: 0.01 us -> 5.21 us  [on_device(): other = lax.ppermute(jnp.where(first, high, low), 'vol', [(0, 1), (1, 0)])]
  transfers between devices with their start and end apart: 2 -> 2, of which waited for: 2 -> 2; matrix products, arithmetic and copies ran while one was open for 3% -> 17% of each run, Pallas kernels for 0% -> 0%
where the time goes in v1:
time: 116 us
  blocking collectives  40.1 us (35%)
  waiting for transfers between devices  31.3 us (27%)
  matrix products  14.7 us (13%)
  between operations  14.2 us (12%)
  local copies, waits for them, and re-layouts  7.81 us (7%)
  other arithmetic  7.68 us (7%)
    all_gather x1, blocking collectives, on_device(): all_spread = lax.all_gather(spread, 'ptcl', axis=0, tiled=True)  36.3 us
    all_gather x1, waiting for transfers between devices, on_device(): all_images = lax.all_gather(images, 'ptcl', axis=0, tiled=True)  27.7 us
    select_n x1, other arithmetic, on_device(): other = lax.ppermute(jnp.where(first, high, low), 'vol', [(0, 1), (1, 0)])  5.21 us
    dot_general x1, matrix products, on_device(): lax.dot_general(all_spread, all_images, (((0,), (0,)), ((), ())), preferr...  4.78 us
    dot_general x1, matrix products, on_device(): jnp.einsum('ok,ckp->cop', table_other, other, preferred_element_type=jnp....  4.64 us
    unnamed x11, local copies, waits for them, and re-layouts  3.86 us
    psum x1, blocking collectives, on_device(): sel = lax.psum(sel, 'vol')  3.72 us
    convert_element_type x1, local copies, waits for them, and re-layouts, on_device(): projection = (jnp.einsum('ok,ckp->cop', table_mine, mine, preferred_eleme...  3.34 us
  transfers between devices with their start and end apart: 2, of which 2 were waited for; matrix products, arithmetic and copies ran while one was open for 17% of the time, Pallas kernels for 0%

profile of v1, /device:TPU:0, one launch (start us, length us, event | category | flops | bytes accessed | tf_op | source)
XLA Modules:
  0.0 116.2 jit_solution(10313928051148906208)
XLA Ops:
  7.2 0.0 all-gather.2.cloned.1.call-start
  7.2 0.7 all-gather.2.cloned.1.call-update
  7.9 0.0 copy-start.1
  7.9 0.0 copy-start.2
  7.9 0.0 copy-start
  7.9 5.2 %broadcast_select_fusion = (bf16[4,90,2880]{2,0,1:T(4,128)(2,1)}, bf16[4,90,2880]{2,0,1:T(4,128)(2,1)S(1)}) fusion(pred[]{:T(512)S(6)} %eq.263, bf16[4,90,5760]{2,0,1:T(4,128)(2,1)} %param.6), kind=kLoop, calls=%fused_computation.13 | loop fusion | flops 2073600 | bytes 8294401 | tf_op jit(solution)/shard_map/jit(_where)/select_n | solution.py:56
  13.1 0.5 collective-permute-start
  13.6 0.0 copy-done.1
  13.6 0.1 copy.32
  13.7 0.0 copy-done.2
  13.7 0.1 copy.36
  13.8 0.0 copy-done
  13.8 1.0 fusion.5
  14.8 2.9 %collective-permute-done = bf16[4,90,2880]{2,0,1:T(4,128)(2,1)} collective-permute-done((bf16[4,90,2880]{2,0,1:T(4,128)(2,1)}, bf16[4,90,2880]{2,0,1:T(4,128)(2,1)}, u32[]{:S(2)}, u32[]{:S(2)}) %collective-permute-start) | collective-permute-done | bytes 2073632 | tf_op jit(solution)/shard_map/ppermute | solution.py:56
  17.8 4.6 %multiply_reduce_fusion = (f32[4,128]{1,0:T(4,128)S(1)}, bf16[4,128,2880]{1,2,0:T(8,128)(2,1)}) fusion(f32[4,2880,128]{2,1,0:T(8,128)S(1)} %fusion.5, pred[]{:T(512)S(6)} %eq.263, bf16[128,180]{0,1:T(8,128)(2,1)S(1)} %copy-done, bf16[4,90,2880]{2,0,1:T(4,128)(2,1)} %collective-permute-done), kind=kOutput, calls=%fused_computation.1 | convolution fusion | flops 272804608 | bytes 10972161 | tf_op jit(solution)/shard_map/ok,ckp->cop/dot_general | solution.py:61
  22.4 3.3 %copy.35 = bf16[4,128,2880]{2,1,0:T(8,128)(2,1)S(1)} copy(bf16[4,128,2880]{1,2,0:T(8,128)(2,1)} %get-tuple-element.47) | data formatting | bytes 5898240 | tf_op jit(solution)/shard_map/convert_element_type | solution.py:62
  25.7 0.0 copy-start.3
  25.8 2.1 %subtract_bitcast_fusion = f32[96,512]{1,0:T(8,128)S(1)} fusion(f32[512]{0:T(512)S(1)} %multiply_bitcast_fusion, bf16[512,2880]{1,0:T(8,128)(2,1)S(1)} %bitcast.64, bf16[96,2880]{1,0:T(8,128)(2,1)} %param.8), kind=kOutput, calls=%fused_computation.34 | convolution fusion | flops 283164672 | bytes 3700736 | tf_op jit(solution)/shard_map/dot_general | solution.py:65
  27.9 0.6 select_reduce_fusion
  28.5 3.7 %psum.7 = f32[96,16]{1,0:T(8,128)S(1)} all-reduce(f32[96,16]{1,0:T(8,128)S(1)} %select_reduce_fusion), channel_id=1, replica_groups=mesh['groups'=2,'ptcl'=8,'vol'=2] {'vol'}, use_global_device_ids=true, to_apply=%region_2.3 | all-reduce | flops 1536 | bytes 12288 | tf_op jit(solution)/shard_map/psum | solution.py:69
  32.2 0.0 copy-done.3
  32.3 0.2 fusion.24
  32.4 0.2 fusion.12
  32.6 0.1 fusion.11
  32.8 0.6 slice_reduce_fusion.15
  33.4 0.7 add_convert_fusion.1
  34.0 36.3 %all_gather.6 = bf16[768,512]{1,0:T(8,128)(2,1)S(1)} all-gather(bf16[96,512]{1,0:T(8,128)(2,1)S(1)} %add_convert_fusion.1), channel_id=1, replica_groups=mesh['groups'=2,'ptcl'=8,'vol'=2] {'ptcl'}, dimensions={0}, use_global_device_ids=true | all-gather | bytes 884736 | tf_op jit(solution)/shard_map/all_gather | solution.py:73
  70.4 0.2 convert_reduce_fusion
  70.5 0.5 log_add_fusion
  71.0 0.2 convolution_add_fusion
  71.3 27.7 %all-gather.2.cloned.1.call-done = bf16[768,2880]{1,0:T(8,128)(2,1)} async-done(((bf16[96,2880]{1,0:T(8,128)(2,1)}), bf16[768,2880]{1,0:T(8,128)(2,1)}) %all-gather.2.cloned.1.call-update) | async-done | bytes 4423696 | tf_op jit(solution)/shard_map/all_gather | solution.py:52
  98.9 4.8 %fusion.7 = bf16[360,4,8,128]{3,2,1,0:T(8,128)(2,1)S(1)} fusion(bf16[768,512]{1,0:T(8,128)(2,1)S(1)} %all_gather.6, bf16[768,2880]{1,0:T(8,128)(2,1)} %all-gather.2.cloned.1.call-done), kind=kOutput, calls=%fused_computation.15 | convolution fusion | flops 2266398720 | bytes 8159232 | tf_op jit(solution)/shard_map/dot_general | solution.py:74
  103.7 1.9 %fusion = bf16[4,180,2880]{2,1,0:T(8,128)(2,1)S(1)} fusion(f32[4,180]{1,0:T(4,128)S(1)} %convolution_add_fusion, bf16[360,4,8,128]{3,2,1,0:T(8,128)(2,1)S(1)} %fusion.7, bf16[128,180]{0,1:T(8,128)(2,1)S(1)} %copy-done), kind=kOutput, calls=%fused_computation.4 | convolution fusion | flops 534988800 | bytes 7145280 | tf_op jit(solution)/shard_map/ok,cop->ckp/dot_general | solution.py:34
  105.7 3.7 %copy.38 = bf16[4,180,2880]{2,0,1:T(4,128)(2,1)} copy(bf16[4,180,2880]{2,1,0:T(8,128)(2,1)S(1)} %fusion) | data formatting | bytes 8294400
  (2 shorter events, 0.0 us)
Async XLA Ops:
  7.2 91.8 %all-gather.2.cloned.1.call-start = ((), (), s32[]{:S(2)}) async-start(), calls=%async_computation | async-start | bytes 5087232 | tf_op jit(solution)/shard_map/all_gather | solution.py:52
  7.9 5.7 %copy-start.1 = (s32[96,16]{0,1:T(8,128)S(1)}, s32[96,16]{0,1:T(8,128)}, u32[]{:S(2)}) copy-start(s32[96,16]{0,1:T(8,128)} %param.10) | copy-start | bytes 18436
  7.9 5.8 %copy-start.2 = (f32[96,16]{0,1:T(8,128)S(1)}, f32[96,16]{0,1:T(8,128)}, u32[]{:S(2)}) copy-start(f32[96,16]{0,1:T(8,128)} %param.9) | copy-start | bytes 18436
  7.9 5.9 %copy-start = (bf16[128,180]{0,1:T(8,128)(2,1)S(1)}, bf16[128,180]{0,1:T(8,128)(2,1)}, u32[]{:S(2)}) copy-start(bf16[128,180]{0,1:T(8,128)(2,1)} %param.7) | copy-start | bytes 138244
  13.1 4.6 %collective-permute-start = (bf16[4,90,2880]{2,0,1:T(4,128)(2,1)}, bf16[4,90,2880]{2,0,1:T(4,128)(2,1)}, u32[]{:S(2)}, u32[]{:S(2)}) collective-permute-start(bf16[4,90,2880]{2,0,1:T(4,128)(2,1)} %get-tuple-element.28), channel_id=1, source_target_pairs={{0,1},{1,0},{2,3},{3,2},{4,5},{5,4},{6,7},{7,6},{8,9},{9,8},{10,11... | collective-permute-start | bytes 6220808 | tf_op jit(solution)/shard_map/ppermute | solution.py:56
  25.7 6.5 %copy-start.3 = (s32[96]{0:T(128)S(1)}, s32[96]{0:T(128)}, u32[]{:S(2)}) copy-start(s32[96]{0:T(128)} %param.11) | copy-start | bytes 1156
Sparse Core Ops, SparseCore 0:
  10.2 88.7 all-gather.1

commit v2 on v0

v2 whole, which is shorter than its diff:
```python
import functools
import math

import jax
import jax.numpy as jnp
from jax import lax
from jax.experimental import pallas as pl
from jax.experimental.pallas import tpu as pltpu
from jax.sharding import PartitionSpec as P

MESH = pl.DeviceIdType.MESH
UP, DOWN, SIDE = 0, 1, 2
VMEM_LIMIT = 56 * 1024 * 1024


def grid_of(members):
    return (4, 2) if members == 8 else (members, 1)


def pieces_of(rows, pairs):
    if pairs == 1 or rows % 16 or rows < 48:
        return [(0, rows)] if pairs == 1 else [(0, 0), (0, rows)]
    first = 16
    half = (rows - first) // 32 * 16
    return [(0, first), (first, rows - first - half), (rows - half, half)]


def gather_kernel(
    members, width, score_scale,
    slabs, table, images, padded, offsets, lists, counts,
    rows_out, totals_out, norm_out,
    own_slab, peer_slab, gathered, acc, joint, part, notes,
    own_sem, slab_send, slab_recv, part_send, part_recv, note_send, note_recv, send_sem, recv_sem,
):
    line, pairs = grid_of(members)
    me = lax.axis_index("ptcl")
    vol = lax.axis_index("vol")
    z, y = me // pairs, me % pairs
    classes, kz_dev, pixels = slabs.shape
    orients = table.shape[0]
    rows, half = images.shape
    slots = offsets.shape[0]
    shift = pixels - width

    barrier = pltpu.get_barrier_semaphore()
    for k in range(1, members):
        pl.semaphore_signal(barrier, inc=1, device_id={"ptcl": (me + k) % members}, device_id_type=MESH)
    pl.semaphore_signal(barrier, inc=1, device_id={"vol": 1 - vol}, device_id_type=MESH)

    own_copies = []
    for c in range(classes):
        copy = pltpu.make_async_copy(
            slabs.at[c, :, pl.ds(pl.multiple_of(vol * shift, 128), width)], own_slab.at[c], own_sem.at[c]
        )
        copy.start()
        own_copies.append(copy)
    pl.semaphore_wait(barrier, members)

    parts = pieces_of(rows, pairs)
    early = 0 if pairs == 2 else -1

    def hop(way, piece, origin, source):
        start, size = parts[piece]
        if way == SIDE:
            target = z * pairs + (1 - y)
        else:
            target = (z + (1 if way == UP else -1)) * pairs + y
            target = jnp.clip(target, 0, members - 1)
        return pltpu.make_async_remote_copy(
            src_ref=source.at[pl.ds(start, size), :],
            dst_ref=gathered.at[origin, pl.ds(start, size), :],
            send_sem=send_sem.at[way, piece, origin],
            recv_sem=recv_sem.at[piece, origin],
            device_id={"ptcl": target},
            device_id_type=MESH,
        )

    def arrived(piece, origin):
        start, size = parts[piece]
        spot = gathered.at[origin, pl.ds(start, size), :]
        pltpu.make_async_copy(spot, spot, recv_sem.at[piece, origin]).wait()

    def relay(way, piece, origin, source):
        @pl.when(z < line - 1 if way == UP else z > 0)
        def _():
            hop(way, piece, origin, source).start()

    slab_copies = []
    for c in range(classes):
        copy = pltpu.make_async_remote_copy(
            src_ref=slabs.at[c, :, pl.ds(pl.multiple_of((1 - vol) * shift, 128), width)],
            dst_ref=peer_slab.at[c],
            send_sem=slab_send.at[c],
            recv_sem=slab_recv.at[c],
            device_id={"vol": 1 - vol},
            device_id_type=MESH,
        )
        copy.start()
        slab_copies.append(copy)
    late = [p for p in range(len(parts)) if p != early]
    if pairs == 2:
        hop(SIDE, early, me, images).start()
    for p in late:
        for way in (UP, DOWN):
            relay(way, p, me, images)
        if pairs == 2:
            hop(SIDE, p, me, images).start()
    if pairs == 2:
        for way in (UP, DOWN):
            relay(way, early, me, images)
    gathered[me] = images[...]

    first = vol == 0
    low, high = table[:, :kz_dev], table[:, kz_dev:]
    table_own = jnp.where(first, low, high)
    table_peer = jnp.where(first, high, low)
    for c in range(classes):
        own_copies[c].wait()
        acc[pl.ds(c * orients, orients), :] = jnp.dot(
            table_own, own_slab[c], preferred_element_type=jnp.float32
        )
    twin = z * pairs + (1 - y)
    if pairs == 2:
        arrived(early, twin)
        for way in (UP, DOWN):
            relay(way, early, twin, gathered.at[twin])

    lane = lax.broadcasted_iota(jnp.int32, (orients, width), 1)
    skip = vol * (width - half)
    inside = (lane >= skip) & (lane < skip + half)
    for c in range(classes):
        slab_copies[c].wait_recv()
        value = acc[pl.ds(c * orients, orients), :] + jnp.dot(
            table_peer, peer_slab[c], preferred_element_type=jnp.float32
        )
        value = jnp.where(inside, value, 0.0).astype(jnp.bfloat16)
        wide = value.astype(jnp.float32)
        power = jnp.sum(wide * wide, axis=1, keepdims=True)
        cross = lax.dot_general(
            value, padded[...], (((1,), (1,)), ((), ())), preferred_element_type=jnp.float32
        )
        joint[pl.ds(c * orients, orients), :] = cross - 0.5 * power

    column = lax.broadcasted_iota(jnp.int32, (classes * orients, rows), 0)
    for s in range(slots):
        hit = column == lists[s : s + 1, :]
        part[0, s : s + 1, :] = jnp.sum(jnp.where(hit, joint[...], 0.0), axis=0, keepdims=True)
    part_copy = pltpu.make_async_remote_copy(
        src_ref=part.at[0],
        dst_ref=part.at[1],
        send_sem=part_send,
        recv_sem=part_recv,
        device_id={"vol": 1 - vol},
        device_id_type=MESH,
    )
    part_copy.start()

    def step(t):
        for way in (UP, DOWN):
            @pl.when(z - 1 - t >= 0 if way == UP else z + 1 + t < line)
            def _():
                far = (z - 1 - t if way == UP else z + 1 + t) * pairs
                for p in late:
                    arrived(p, far + y)
                    relay(way, p, far + y, gathered.at[far + y])
                    if pairs == 2:
                        hop(SIDE, p, far + y, gathered.at[far + y]).start()
                if pairs == 2:
                    for q in range(pairs):
                        arrived(early, far + q)
                        relay(way, early, far + q, gathered.at[far + q])

    def accumulate(origin, fresh=False):
        def block(b, carry):
            base = pl.multiple_of(b * orients, orients)
            target = lax.broadcasted_iota(jnp.int32, (orients, rows), 0) + base
            target = target.astype(jnp.float32)
            note = notes[origin]
            spread = jnp.zeros((orients, rows), jnp.float32)
            for s in range(slots):
                hit = target == note[slots + s : slots + s + 1, :]
                spread = spread + jnp.where(hit, note[s : s + 1, :], 0.0)
            spread = spread.astype(jnp.bfloat16)
            total = jnp.sum(spread.astype(jnp.float32), axis=1, keepdims=True)
            total = jnp.broadcast_to(total, (orients, totals_out.shape[1]))
            value = jnp.dot(spread, gathered[origin], preferred_element_type=jnp.float32)
            spot = pl.ds(base, orients)
            if fresh:
                totals_out[spot, :] = total
                acc[spot, :half] = value
            else:
                totals_out[spot, :] += total
                acc[spot, :half] += value
            return carry

        lax.fori_loop(0, classes, block, 0)

    def note_arrived(origin):
        pltpu.make_async_copy(notes.at[origin], notes.at[origin], note_recv.at[origin]).wait()

    step(0)

    part_copy.wait_recv()
    scores = score_scale * (part[0] + part[1]) + offsets[...]
    slot = lax.broadcasted_iota(jnp.int32, (slots, rows), 0)
    live = slot < counts[...]
    masked = jnp.where(live, scores, -1e30)
    top = jnp.max(masked, axis=0, keepdims=True)
    expon = jnp.where(live, jnp.exp(masked - top), 0.0)
    whole = jnp.sum(expon, axis=0, keepdims=True)
    norm_out[...] = top + jnp.log(whole)
    notes[me, :slots, :] = expon / whole
    notes[me, slots:, :] = lists[...].astype(jnp.float32)
    note_copies = []
    for k in range(1, members):
        copy = pltpu.make_async_remote_copy(
            src_ref=notes.at[me],
            dst_ref=notes.at[me],
            send_sem=note_send.at[k],
            recv_sem=note_recv.at[me],
            device_id={"ptcl": (me + k) % members},
            device_id_type=MESH,
        )
        copy.start()
        note_copies.append(copy)
    accumulate(me, fresh=True)

    def add_pair(origin):
        note_arrived(origin)
        accumulate(origin)

    def add_twin(origin):
        for p in late:
            arrived(p, origin)
        note_arrived(origin)
        accumulate(origin)

    def settle(t):
        for way in (UP, DOWN):
            @pl.when(z - 1 - t >= 0 if way == UP else z + 1 + t < line)
            def _():
                add_pair((z - 1 - t if way == UP else z + 1 + t) * pairs + y)

    def settle_twin(t):
        for way in (UP, DOWN):
            @pl.when(z - 1 - t >= 0 if way == UP else z + 1 + t < line)
            def _():
                add_twin((z - 1 - t if way == UP else z + 1 + t) * pairs + (1 - y))

    for t in range(1, line - 1):
        step(t)
        if t == 1 and pairs == 2:
            add_twin(twin)
        settle(t - 1)
        if pairs == 2 and t >= 2:
            settle_twin(t - 2)
    settle(line - 2)
    if pairs == 2:
        for t in range(max(0, line - 3), line - 1):
            settle_twin(t)
    for c in range(classes):
        spot = pl.ds(c * orients, orients)
        rows_out[spot, :] = acc[spot, :half].astype(jnp.bfloat16)

    for copy in slab_copies + [part_copy] + note_copies:
        copy.wait_send()

    for way in (UP, DOWN):
        @pl.when(z < line - 1 if way == UP else z > 0)
        def _():
            for t in range(-1, line - 1):
                origin_z = z - 1 - t if way == UP else z + 1 + t

                @pl.when(origin_z >= 0 if way == UP else origin_z < line)
                def _():
                    for p in late:
                        hop(way, p, origin_z * pairs + y, images).wait_send()
                    if pairs == 2:
                        for q in range(pairs):
                            hop(way, early, origin_z * pairs + q, images).wait_send()
    if pairs == 2:
        hop(SIDE, early, me, images).wait_send()
        for other in range(line):
            for p in late:
                hop(SIDE, p, other * pairs + y, images).wait_send()


def back_kernel(table, rows, totals, out):
    kernel = table[...].astype(jnp.float32)
    below = 1.0 + lax.dot_general(
        kernel * kernel,
        totals[...],
        (((0,), (0,)), ((), ())),
        precision=lax.Precision.HIGHEST,
        preferred_element_type=jnp.float32,
    )[:, :1]
    above = lax.dot_general(
        table[...], rows[...], (((0,), (0,)), ((), ())), preferred_element_type=jnp.float32
    )
    out[0] = (above / below).astype(jnp.bfloat16)


def on_device(reference_slabs, slice_table, images, offsets, orient_lists, counts):
    classes, kz_dev, pixels = reference_slabs.shape
    orients, planes = slice_table.shape
    columns = classes * orients
    rows, half = images.shape
    slots = offsets.shape[1]
    members = lax.axis_size("ptcl")
    line, pairs = grid_of(members)
    parts = pieces_of(rows, pairs)
    width = pixels - half // 128 * 128
    spare = width - half
    padded = jnp.where(
        lax.axis_index("vol") == 0,
        jnp.pad(images, ((0, 0), (0, spare))),
        jnp.pad(images, ((0, 0), (spare, 0))),
    )
    score_scale = 4.0 / math.sqrt(pixels)
    vmem = pl.BlockSpec(memory_space=pltpu.VMEM)
    dma = pltpu.SemaphoreType.DMA
    sum_rows, totals, log_norm = pl.pallas_call(
        functools.partial(gather_kernel, members, width, score_scale),
        out_shape=(
            jax.ShapeDtypeStruct((columns, half), jnp.bfloat16),
            jax.ShapeDtypeStruct((columns, 128), jnp.float32),
            jax.ShapeDtypeStruct((1, rows), jnp.float32),
        ),
        in_specs=[pl.BlockSpec(memory_space=pl.ANY)] + [vmem] * 6,
        out_specs=(vmem, vmem, vmem),
        scratch_shapes=[
            pltpu.VMEM((classes, kz_dev, width), jnp.bfloat16),
            pltpu.VMEM((classes, kz_dev, width), jnp.bfloat16),
            pltpu.VMEM((members, rows, half), jnp.bfloat16),
            pltpu.VMEM((columns, width), jnp.float32),
            pltpu.VMEM((columns, rows), jnp.float32),
            pltpu.VMEM((2, slots, rows), jnp.float32),
            pltpu.VMEM((members, 2 * slots, rows), jnp.float32),
            dma((classes,)),
            dma((classes,)),
            dma((classes,)),
            dma,
            dma,
            dma((members,)),
            dma((members,)),
            dma((3, len(parts), members)),
            dma((len(parts), members)),
        ],
        compiler_params=pltpu.CompilerParams(
            collective_id=0, has_side_effects=True, vmem_limit_bytes=VMEM_LIMIT
        ),
        name="gather_and_sum",
    )(reference_slabs, slice_table, images, padded, offsets.T, orient_lists.T, counts[None, :])
    new_ref = pl.pallas_call(
        back_kernel,
        grid=(classes,),
        out_shape=jax.ShapeDtypeStruct((classes, planes, half), jnp.bfloat16),
        in_specs=[
            pl.BlockSpec((orients, planes), lambda c: (0, 0)),
            pl.BlockSpec((orients, half), lambda c: (c, 0)),
            pl.BlockSpec((orients, 128), lambda c: (c, 0)),
        ],
        out_specs=pl.BlockSpec((1, planes, half), lambda c: (c, 0, 0)),
        compiler_params=pltpu.CompilerParams(vmem_limit_bytes=VMEM_LIMIT),
        name="back_project",
    )(slice_table, sum_rows, totals)
    return (new_ref, log_norm[0])


def solution(mesh):
    placed = (
        P("groups", "vol", None),
        P(),
        P(("groups", "ptcl"), "vol"),
        P(("groups", "ptcl"), None),
        P(("groups", "ptcl"), None),
        P(("groups", "ptcl")),
    )
    return jax.shard_map(
        on_device,
        mesh=mesh,
        in_specs=placed,
        out_specs=(P("groups", None, "vol"), P(("groups", "ptcl"))),
        check_vma=False,
    )
```

time: 349 us -> 88 us (0.25)
  blocking collectives: 238 us -> 0 us
  Pallas kernels: 0 us -> 72.1 us
  local copies, waits for them, and re-layouts: 43.5 us -> 12.5 us
  waiting for transfers between devices: 29.7 us -> 0 us
  matrix products: 19.9 us -> 0 us
  between operations: 14.2 us -> 0.65 us
    psum x2 -> x0, blocking collectives: 238 us -> none  [the longest x1 235 us: on_device(): sum_rows, totals = lax.psum((row_part, total_part), 'ptcl')]
    pallas_call x0 -> x2, Pallas kernels: none -> 72.1 us  [the longest x1 66.1 us: on_device(): pl.pallas_call(functools.partial(gather_kernel, members, width, score_sca...]
    unnamed x3 -> x0, waiting for transfers between devices: 22.3 us -> none
    gather x6 -> x0, local copies, waits for them, and re-layouts: 21.3 us -> none  [the longest x5 11.8 us: on_device(): sel_cross = jnp.take_along_axis(crossed, orient_lists, axis=1)]
    dot_general x5 -> x0, matrix products: 19.9 us -> none  [the longest x1 8.25 us: on_device(): jnp.einsum('ckp,ok->pco', reference_slabs, table_local, preferred_element...]
    unnamed x13 -> x6, local copies, waits for them, and re-layouts: 21.8 us -> 12.5 us
    psum x1 -> x0, waiting for transfers between devices: 7.38 us -> none  [on_device(): crossed, powers = lax.psum((cross_part, power_part), 'vol')]
  transfers between devices with their start and end apart: 2 -> 0, of which waited for: 2 -> 0; matrix products, arithmetic and copies ran while one was open for 3% -> 0% of each run, Pallas kernels for 0% -> 0%
where the time goes in v2:
time: 88 us; the launch traced here: 87.6 us
  Pallas kernels  72.1 us (82%)
  local copies, waits for them, and re-layouts  12.5 us (14%)
  other arithmetic  2.33 us (3%)
    pallas_call x1, Pallas kernels, on_device(): pl.pallas_call(functools.partial(gather_kernel, members, width, score_sca...  66.1 us
    unnamed x6, local copies, waits for them, and re-layouts  12.5 us
    pallas_call x1, Pallas kernels, on_device(): pl.pallas_call(back_kernel, grid=(classes,), out_shape=jax.ShapeDtypeStru...  5.95 us
    select_n x1, other arithmetic, on_device(): jnp.where(lax.axis_index('vol') == 0, jnp.pad(images, ((0, 0), (0, spare)...  2.33 us

profile of v2, /device:TPU:0, one launch (start us, length us, event | category | flops | bytes accessed | tf_op | source)
XLA Modules:
  0.0 87.6 jit_solution(14716464268740736628)
XLA Ops:
  0.6 1.5 %copy.10.table = bf16[128,180]{1,0:T(8,128)(2,1)} copy(bf16[128,180]{0,1:T(8,128)(2,1)} %param.7) | data formatting | bytes 92160 | tf_op args[1]
  2.1 2.3 %pad_select_fusion.padded = bf16[96,2944]{1,0:T(8,128)(2,1)} fusion(bf16[96,2880]{1,0:T(8,128)(2,1)} %images.1, pred[]{:T(512)S(6)} %eq.3), kind=kLoop, calls=%fused_computation | loop fusion | flops 282624 | bytes 1118209 | tf_op jit(solution)/shard_map/jit(_where)/select_n | solution.py:314
  4.5 4.6 %copy.8.slabs = bf16[4,90,5760]{2,1,0:T(8,128)(2,1)} copy(bf16[4,90,5760]{2,0,1:T(4,128)(2,1)} %param.6) | data formatting | bytes 8294400 | tf_op args[0]
  9.1 66.1 %gather_and_sum.1 = (bf16[512,2880]{1,0:T(8,128)(2,1)}, f32[512,128]{1,0:T(8,128)}, f32[1,96]{1,0:T(1,128)}) custom-call(bf16[4,90,5760]{2,1,0:T(8,128)(2,1)} %copy.8.slabs, bf16[128,180]{1,0:T(8,128)(2,1)} %copy.10.table, bf16[96,2880]{1,0:T(8,128)(2,1)} %images.1, bf16[96,2944]{1,0:T(8,128)(2,1)} %pad_select_fusion.padded, f32[16,96]{1,0:T(8,128)} %bitcast.4, ...), custom_call_target="tpu_custom_call" | custom-call | tf_op jit(solution)/shard_map/gather_and_sum/pallas_call | solution.py:322
  75.3 5.9 %back_project.1 = bf16[4,180,2880]{2,1,0:T(8,128)(2,1)} custom-call(bf16[128,180]{1,0:T(8,128)(2,1)} %copy.10.table, bf16[512,2880]{1,0:T(8,128)(2,1)} %get-tuple-element.5.rows, f32[512,128]{1,0:T(8,128)} %get-tuple-element.6.totals), custom_call_target="tpu_custom_call" | custom-call | tf_op jit(solution)/shard_map/back_project/pallas_call | solution.py:354
  81.2 0.0 copy-start
  81.2 5.9 %copy.11 = bf16[4,180,2880]{2,0,1:T(4,128)(2,1)} copy(bf16[4,180,2880]{2,1,0:T(8,128)(2,1)} %back_project.1) | data formatting | bytes 8294400
  87.1 0.0 copy-done
  87.1 0.5 copy.13
Async XLA Ops:
  81.2 5.9 %copy-start = (f32[1,96]{1,0:T(1,128)S(1)}, f32[1,96]{1,0:T(1,128)}, u32[]{:S(2)}) copy-start(f32[1,96]{1,0:T(1,128)} %get-tuple-element.7) | copy-start | bytes 1156

commit v3 on v2

--- a/solution.py
+++ b/solution.py
@@ -27,17 +27,17 @@
 
 def gather_kernel(
     members, width, score_scale,
-    slabs, table, images, padded, offsets, lists, counts,
+    slabs, planes_table, images, offsets, lists, counts,
     rows_out, totals_out, norm_out,
-    own_slab, peer_slab, gathered, acc, joint, part, notes,
+    own_slab, peer_slab, flat, spans, padded, gathered, acc, joint, part, notes,
     own_sem, slab_send, slab_recv, part_send, part_recv, note_send, note_recv, send_sem, recv_sem,
 ):
     line, pairs = grid_of(members)
     me = lax.axis_index("ptcl")
     vol = lax.axis_index("vol")
     z, y = me // pairs, me % pairs
-    classes, kz_dev, pixels = slabs.shape
-    orients = table.shape[0]
+    kz_dev, classes, pixels = slabs.shape
+    planes, orients = planes_table.shape
     rows, half = images.shape
     slots = offsets.shape[0]
     shift = pixels - width
@@ -47,13 +47,10 @@
         pl.semaphore_signal(barrier, inc=1, device_id={"ptcl": (me + k) % members}, device_id_type=MESH)
     pl.semaphore_signal(barrier, inc=1, device_id={"vol": 1 - vol}, device_id_type=MESH)
 
-    own_copies = []
-    for c in range(classes):
-        copy = pltpu.make_async_copy(
-            slabs.at[c, :, pl.ds(pl.multiple_of(vol * shift, 128), width)], own_slab.at[c], own_sem.at[c]
-        )
-        copy.start()
-        own_copies.append(copy)
+    own_copy = pltpu.make_async_copy(
+        slabs.at[:, :, pl.ds(pl.multiple_of(vol * shift, 128), width)], own_slab, own_sem
+    )
+    own_copy.start()
     pl.semaphore_wait(barrier, members)
 
     parts = pieces_of(rows, pairs)
@@ -85,18 +82,15 @@
         def _():
             hop(way, piece, origin, source).start()
 
-    slab_copies = []
-    for c in range(classes):
-        copy = pltpu.make_async_remote_copy(
-            src_ref=slabs.at[c, :, pl.ds(pl.multiple_of((1 - vol) * shift, 128), width)],
-            dst_ref=peer_slab.at[c],
-            send_sem=slab_send.at[c],
-            recv_sem=slab_recv.at[c],
-            device_id={"vol": 1 - vol},
-            device_id_type=MESH,
-        )
-        copy.start()
-        slab_copies.append(copy)
+    slab_copy = pltpu.make_async_remote_copy(
+        src_ref=slabs.at[:, :, pl.ds(pl.multiple_of((1 - vol) * shift, 128), width)],
+        dst_ref=peer_slab,
+        send_sem=slab_send,
+        recv_sem=slab_recv,
+        device_id={"vol": 1 - vol},
+        device_id_type=MESH,
+    )
+    slab_copy.start()
     late = [p for p in range(len(parts)) if p != early]
     if pairs == 2:
         hop(SIDE, early, me, images).start()
@@ -110,36 +104,62 @@
             relay(way, early, me, images)
     gathered[me] = images[...]
 
-    first = vol == 0
-    low, high = table[:, :kz_dev], table[:, kz_dev:]
-    table_own = jnp.where(first, low, high)
-    table_peer = jnp.where(first, high, low)
-    for c in range(classes):
-        own_copies[c].wait()
-        acc[pl.ds(c * orients, orients), :] = jnp.dot(
-            table_own, own_slab[c], preferred_element_type=jnp.float32
-        )
+    pair = lax.broadcasted_iota(jnp.int32, (planes, kz_dev * classes), 1)
+    plane = lax.broadcasted_iota(jnp.int32, (planes, kz_dev * classes), 0)
+    of_class = lax.broadcasted_iota(jnp.int32, (orients, kz_dev * classes), 1) % classes
+    for side, which in enumerate((vol, 1 - vol)):
+        pick = jnp.where(plane == pair // classes + which * kz_dev, 1.0, 0.0).astype(jnp.bfloat16)
+        repeated = lax.dot_general(
+            planes_table[...], pick, (((0,), (0,)), ((), ())), preferred_element_type=jnp.float32
+        )
+        for c in range(classes):
+            spans[side, c * orients : (c + 1) * orients, :] = jnp.where(
+                of_class == c, repeated, 0.0
+            ).astype(jnp.bfloat16)
+
+    @pl.when(vol == 0)
+    def _():
+        padded[:, :half] = images[...]
+        padded[:, half:] = jnp.zeros((rows, width - half), jnp.bfloat16)
+
+    @pl.when(vol != 0)
+    def _():
+        padded[:, width - half :] = images[...]
+        padded[:, : width - half] = jnp.zeros((rows, width - half), jnp.bfloat16)
+
+    own_copy.wait()
+    flat[0] = own_slab[...].reshape(kz_dev * classes, width)
     twin = z * pairs + (1 - y)
     if pairs == 2:
         arrived(early, twin)
         for way in (UP, DOWN):
             relay(way, early, twin, gathered.at[twin])
 
-    lane = lax.broadcasted_iota(jnp.int32, (orients, width), 1)
+    slab_copy.wait_recv()
+    flat[1] = peer_slab[...].reshape(kz_dev * classes, width)
     skip = vol * (width - half)
-    inside = (lane >= skip) & (lane < skip + half)
-    for c in range(classes):
-        slab_copies[c].wait_recv()
-        value = acc[pl.ds(c * orients, orients), :] + jnp.dot(
-            table_peer, peer_slab[c], preferred_element_type=jnp.float32
-        )
-        value = jnp.where(inside, value, 0.0).astype(jnp.bfloat16)
+    power = jnp.zeros((classes * orients, 1), jnp.float32)
+    for start in range(0, width, 1024):
+        size = min(1024, width - start)
+        value = jnp.dot(spans[0], flat[0, :, start : start + size], preferred_element_type=jnp.float32)
+        value = value + jnp.dot(
+            spans[1], flat[1, :, start : start + size], preferred_element_type=jnp.float32
+        )
+        lane = lax.broadcasted_iota(jnp.int32, (classes * orients, size), 1) + start
+        value = jnp.where((lane >= skip) & (lane < skip + half), value, 0.0).astype(jnp.bfloat16)
         wide = value.astype(jnp.float32)
-        power = jnp.sum(wide * wide, axis=1, keepdims=True)
+        power = power + jnp.sum(wide * wide, axis=1, keepdims=True)
         cross = lax.dot_general(
-            value, padded[...], (((1,), (1,)), ((), ())), preferred_element_type=jnp.float32
-        )
-        joint[pl.ds(c * orients, orients), :] = cross - 0.5 * power
+            value,
+            padded[:, start : start + size],
+            (((1,), (1,)), ((), ())),
+            preferred_element_type=jnp.float32,
+        )
+        if start == 0:
+            joint[...] = cross
+        else:
+            joint[...] += cross
+    joint[...] -= 0.5 * power
 
     column = lax.broadcasted_iota(jnp.int32, (classes * orients, rows), 0)
     for s in range(slots):
@@ -262,7 +282,7 @@
         spot = pl.ds(c * orients, orients)
         rows_out[spot, :] = acc[spot, :half].astype(jnp.bfloat16)
 
-    for copy in slab_copies + [part_copy] + note_copies:
+    for copy in [slab_copy, part_copy] + note_copies:
         copy.wait_send()
 
     for way in (UP, DOWN):
@@ -285,19 +305,27 @@
                 hop(SIDE, p, other * pairs + y, images).wait_send()
 
 
-def back_kernel(table, rows, totals, out):
-    kernel = table[...].astype(jnp.float32)
-    below = 1.0 + lax.dot_general(
-        kernel * kernel,
-        totals[...],
-        (((0,), (0,)), ((), ())),
-        precision=lax.Precision.HIGHEST,
-        preferred_element_type=jnp.float32,
-    )[:, :1]
-    above = lax.dot_general(
-        table[...], rows[...], (((0,), (0,)), ((), ())), preferred_element_type=jnp.float32
-    )
-    out[0] = (above / below).astype(jnp.bfloat16)
+def back_kernel(planes_table, rows, totals, out):
+    part, classes, half = out.shape
+    planes, orients = planes_table.shape
+    pair = lax.broadcasted_iota(jnp.int32, (part * classes, planes), 0)
+    plane = lax.broadcasted_iota(jnp.int32, (part * classes, planes), 1)
+    pick = jnp.where(plane == pair // classes + pl.program_id(0) * part, 1.0, 0.0).astype(jnp.bfloat16)
+    repeated = jnp.dot(pick, planes_table[...], preferred_element_type=jnp.float32)
+    of_class = lax.broadcasted_iota(jnp.int32, (part * classes, orients), 0) % classes
+    blocks = []
+    below = 1.0
+    for c in range(classes):
+        block = jnp.where(of_class == c, repeated, 0.0)
+        below = below + jnp.dot(
+            block * block,
+            totals[c * orients : (c + 1) * orients, :],
+            precision=lax.Precision.HIGHEST,
+            preferred_element_type=jnp.float32,
+        )
+        blocks.append(block.astype(jnp.bfloat16))
+    above = jnp.dot(jnp.concatenate(blocks, axis=1), rows[...], preferred_element_type=jnp.float32)
+    out[...] = (above / below[:, :1]).astype(jnp.bfloat16).reshape(part, classes, half)
 
 
 def on_device(reference_slabs, slice_table, images, offsets, orient_lists, counts):
@@ -310,12 +338,8 @@
     line, pairs = grid_of(members)
     parts = pieces_of(rows, pairs)
     width = pixels - half // 128 * 128
-    spare = width - half
-    padded = jnp.where(
-        lax.axis_index("vol") == 0,
-        jnp.pad(images, ((0, 0), (0, spare))),
-        jnp.pad(images, ((0, 0), (spare, 0))),
-    )
+    planes_table = slice_table.T
+    part = max(d for d in range(1, planes + 1) if planes % d == 0 and (d == planes or d * classes % 16 == 0 and d <= 40))
     score_scale = 4.0 / math.sqrt(pixels)
     vmem = pl.BlockSpec(memory_space=pltpu.VMEM)
     dma = pltpu.SemaphoreType.DMA
@@ -326,19 +350,22 @@
             jax.ShapeDtypeStruct((columns, 128), jnp.float32),
             jax.ShapeDtypeStruct((1, rows), jnp.float32),
         ),
-        in_specs=[pl.BlockSpec(memory_space=pl.ANY)] + [vmem] * 6,
+        in_specs=[pl.BlockSpec(memory_space=pl.ANY)] + [vmem] * 5,
         out_specs=(vmem, vmem, vmem),
         scratch_shapes=[
-            pltpu.VMEM((classes, kz_dev, width), jnp.bfloat16),
-            pltpu.VMEM((classes, kz_dev, width), jnp.bfloat16),
+            pltpu.VMEM((kz_dev, classes, width), jnp.bfloat16),
+            pltpu.VMEM((kz_dev, classes, width), jnp.bfloat16),
+            pltpu.VMEM((2, kz_dev * classes, width), jnp.bfloat16),
+            pltpu.VMEM((2, columns, kz_dev * classes), jnp.bfloat16),
+            pltpu.VMEM((rows, width), jnp.bfloat16),
             pltpu.VMEM((members, rows, half), jnp.bfloat16),
-            pltpu.VMEM((columns, width), jnp.float32),
+            pltpu.VMEM((columns, half), jnp.float32),
             pltpu.VMEM((columns, rows), jnp.float32),
             pltpu.VMEM((2, slots, rows), jnp.float32),
             pltpu.VMEM((members, 2 * slots, rows), jnp.float32),
-            dma((classes,)),
-            dma((classes,)),
-            dma((classes,)),
+            dma,
+            dma,
+            dma,
             dma,
             dma,
             dma((members,)),
@@ -350,21 +377,19 @@
             collective_id=0, has_side_effects=True, vmem_limit_bytes=VMEM_LIMIT
         ),
         name="gather_and_sum",
-    )(reference_slabs, slice_table, images, padded, offsets.T, orient_lists.T, counts[None, :])
+    )(
+        jnp.swapaxes(reference_slabs, 0, 1), planes_table, images, offsets.T, orient_lists.T, counts[None, :]
+    )
     new_ref = pl.pallas_call(
         back_kernel,
-        grid=(classes,),
-        out_shape=jax.ShapeDtypeStruct((classes, planes, half), jnp.bfloat16),
-        in_specs=[
-            pl.BlockSpec((orients, planes), lambda c: (0, 0)),
-            pl.BlockSpec((orients, half), lambda c: (c, 0)),
-            pl.BlockSpec((orients, 128), lambda c: (c, 0)),
-        ],
-        out_specs=pl.BlockSpec((1, planes, half), lambda c: (c, 0, 0)),
+        grid=(planes // part,),
+        out_shape=jax.ShapeDtypeStruct((planes, classes, half), jnp.bfloat16),
+        in_specs=[vmem, vmem, vmem],
+        out_specs=pl.BlockSpec((part, classes, half), lambda b: (b, 0, 0)),
         compiler_params=pltpu.CompilerParams(vmem_limit_bytes=VMEM_LIMIT),
         name="back_project",
-    )(slice_table, sum_rows, totals)
-    return (new_ref, log_norm[0])
+    )(planes_table, sum_rows, totals)
+    return (jnp.swapaxes(new_ref, 0, 1), log_norm[0])
 
 
 def solution(mesh):

time: 88 us -> 75.2 us (0.85)
  local copies, waits for them, and re-layouts: 12.5 us -> 0.52 us
  other arithmetic: 2.33 us -> 0 us
  Pallas kernels: 72.1 us -> 73.9 us
    unnamed x6 -> x3, local copies, waits for them, and re-layouts: 12.5 us -> 0.52 us
    select_n x1 -> x0, other arithmetic: 2.33 us -> none  [on_device(): jnp.where(lax.axis_index('vol') == 0, jnp.pad(images, ((0, 0), (0, spare)...]
    pallas_call x1, Pallas kernels: 5.95 us -> 8.05 us  [on_device(): pl.pallas_call(back_kernel, grid=(planes // part,), out_shape=jax.ShapeDt...]
where the time goes in v3:
time: 75.2 us; the launch traced here: 75.1 us
  Pallas kernels  73.9 us (98%)
    pallas_call x1, Pallas kernels, on_device(): pl.pallas_call(functools.partial(gather_kernel, members, width, score_sca...  65.9 us
    pallas_call x1, Pallas kernels, on_device(): pl.pallas_call(back_kernel, grid=(planes // part,), out_shape=jax.ShapeDt...  8.05 us

profile of v3, /device:TPU:0, one launch (start us, length us, event | category | flops | bytes accessed | tf_op | source)
XLA Modules:
  0.0 75.1 jit_solution(16836647496778908757)
XLA Ops:
  0.6 65.9 %gather_and_sum.1 = (bf16[512,2880]{1,0:T(8,128)(2,1)}, f32[512,128]{1,0:T(8,128)}, f32[1,96]{1,0:T(1,128)}) custom-call(bf16[90,4,5760]{2,1,0:T(4,128)(2,1)} %bitcast.8, bf16[180,128]{1,0:T(8,128)(2,1)} %bitcast.9, bf16[96,2880]{1,0:T(8,128)(2,1)} %images.1, f32[16,96]{1,0:T(8,128)} %bitcast.11, s32[16,96]{1,0:T(8,128)} %bitcast.12, s32[1,96]{1,0:T(1,128)} %bitcast.13), custom_call_target="tpu_custom_call" | custom-call | tf_op jit(solution)/shard_map/gather_and_sum/pallas_call | solution.py:346
  66.5 0.0 copy-start
  66.5 8.1 %back_project.1 = bf16[180,4,2880]{2,1,0:T(4,128)(2,1)} custom-call(bf16[180,128]{1,0:T(8,128)(2,1)} %bitcast.10, bf16[512,2880]{1,0:T(8,128)(2,1)} %get-tuple-element.5.rows, f32[512,128]{1,0:T(8,128)} %get-tuple-element.6.totals), custom_call_target="tpu_custom_call" | custom-call | tf_op jit(solution)/shard_map/back_project/pallas_call | solution.py:383
  74.6 0.0 copy-done
  74.6 0.5 copy.9
Async XLA Ops:
  66.5 8.1 %copy-start = (f32[1,96]{1,0:T(1,128)S(1)}, f32[1,96]{1,0:T(1,128)}, u32[]{:S(2)}) copy-start(f32[1,96]{1,0:T(1,128)} %get-tuple-element.7) | copy-start | bytes 1156

commit v4 on v3

--- a/solution.py
+++ b/solution.py
@@ -21,8 +21,7 @@
     if pairs == 1 or rows % 16 or rows < 48:
         return [(0, rows)] if pairs == 1 else [(0, 0), (0, rows)]
     first = 16
-    half = (rows - first) // 32 * 16
-    return [(0, first), (first, rows - first - half), (rows - half, half)]
+    return [(0, first)] + [(at, min(32, rows - at)) for at in range(first, rows, 32)]
 
 
 def gather_kernel(
@@ -176,16 +175,20 @@
     part_copy.start()
 
     def step(t):
-        for way in (UP, DOWN):
-            @pl.when(z - 1 - t >= 0 if way == UP else z + 1 + t < line)
-            def _():
-                far = (z - 1 - t if way == UP else z + 1 + t) * pairs
-                for p in late:
+        for p in late:
+            for way in (UP, DOWN):
+                @pl.when(z - 1 - t >= 0 if way == UP else z + 1 + t < line)
+                def _():
+                    far = (z - 1 - t if way == UP else z + 1 + t) * pairs
                     arrived(p, far + y)
                     relay(way, p, far + y, gathered.at[far + y])
                     if pairs == 2:
                         hop(SIDE, p, far + y, gathered.at[far + y]).start()
-                if pairs == 2:
+        if pairs == 2:
+            for way in (UP, DOWN):
+                @pl.when(z - 1 - t >= 0 if way == UP else z + 1 + t < line)
+                def _():
+                    far = (z - 1 - t if way == UP else z + 1 + t) * pairs
                     for q in range(pairs):
                         arrived(early, far + q)
                         relay(way, early, far + q, gathered.at[far + q])
@@ -339,7 +342,7 @@
     parts = pieces_of(rows, pairs)
     width = pixels - half // 128 * 128
     planes_table = slice_table.T
-    part = max(d for d in range(1, planes + 1) if planes % d == 0 and (d == planes or d * classes % 16 == 0 and d <= 40))
+    part = max(d for d in range(1, planes + 1) if planes % d == 0 and (d == planes or d * classes % 16 == 0 and d <= 60))
     score_scale = 4.0 / math.sqrt(pixels)
     vmem = pl.BlockSpec(memory_space=pltpu.VMEM)
     dma = pltpu.SemaphoreType.DMA

time: 75.2 us -> 74.2 us (0.987)
  Pallas kernels: 73.9 us -> 72.9 us
    pallas_call x1, Pallas kernels: 65.9 us -> 64.9 us  [on_device(): pl.pallas_call(functools.partial(gather_kernel, members, width, score_sca...]
where the time goes in v4:
time: 74.2 us; the launch traced here: 74.1 us
  Pallas kernels  72.9 us (98%)
    pallas_call x1, Pallas kernels, on_device(): pl.pallas_call(functools.partial(gather_kernel, members, width, score_sca...  64.9 us
    pallas_call x1, Pallas kernels, on_device(): pl.pallas_call(back_kernel, grid=(planes // part,), out_shape=jax.ShapeDt...  8.05 us

profile of v4, /device:TPU:0, one launch (start us, length us, event | category | flops | bytes accessed | tf_op | source)
XLA Modules:
  0.0 74.1 jit_solution(8382311036489752935)
XLA Ops:
  0.6 64.9 %gather_and_sum.1 = (bf16[512,2880]{1,0:T(8,128)(2,1)}, f32[512,128]{1,0:T(8,128)}, f32[1,96]{1,0:T(1,128)}) custom-call(bf16[90,4,5760]{2,1,0:T(4,128)(2,1)} %bitcast.8, bf16[180,128]{1,0:T(8,128)(2,1)} %bitcast.9, bf16[96,2880]{1,0:T(8,128)(2,1)} %images.1, f32[16,96]{1,0:T(8,128)} %bitcast.11, s32[16,96]{1,0:T(8,128)} %bitcast.12, s32[1,96]{1,0:T(1,128)} %bitcast.13), custom_call_target="tpu_custom_call" | custom-call | tf_op jit(solution)/shard_map/gather_and_sum/pallas_call | solution.py:349
  65.5 0.0 copy-start
  65.5 8.1 %back_project.1 = bf16[180,4,2880]{2,1,0:T(4,128)(2,1)} custom-call(bf16[180,128]{1,0:T(8,128)(2,1)} %bitcast.10, bf16[512,2880]{1,0:T(8,128)(2,1)} %get-tuple-element.5.rows, f32[512,128]{1,0:T(8,128)} %get-tuple-element.6.totals), custom_call_target="tpu_custom_call" | custom-call | tf_op jit(solution)/shard_map/back_project/pallas_call | solution.py:386
  73.6 0.0 copy-done
  73.6 0.5 copy.9
Async XLA Ops:
  65.5 8.1 %copy-start = (f32[1,96]{1,0:T(1,128)S(1)}, f32[1,96]{1,0:T(1,128)}, u32[]{:S(2)}) copy-start(f32[1,96]{1,0:T(1,128)} %get-tuple-element.7) | copy-start | bytes 1156
